TPU v7x, 256 devices: a whole 4x4x8 slice. The times are simulated.
256 devices in a mesh: expert: 2 (over core), group: 64 (over z, y, x_hi), seq: 2 (over x_lo).
Axes of the slice: x: 4 (x_hi: 2, x_lo: 2; x = x_hi * 2 + x_lo), y: 4, z: 8, core: 2. Of those that a mesh axis runs over, the one named last changes fastest.
Arguments:
- latents: bfloat16 [64, 64, 256], P('group', None, 'seq'), may hold values from -6 to 6
- timestep: int32 [64], replicated, may hold values from 0 to 1023
- boundary: int32 [1], replicated, may hold values from 256 to 767
- order: int32 [64], replicated, may hold values from 0 to 63, each once
- lengths: int32 [64], replicated, may hold values from 128 to 256, as said below
- embed_weight: bfloat16 [2, 64, 5120], P('expert'), may hold values from -0.75 to 0.75
- mod_table: float32 [2, 1024, 2, 5120], P('expert', None, None, ('group', 'seq')), may hold values from -3 to 3
- qkv_weight: bfloat16 [2, 5120, 3, 3072], P('expert', None, None, 'seq'), may hold values from -0.078125 to 0.078125
- qk_gain: float32 [2, 2, 3072], P('expert', None, 'seq')
Outputs:
- attended: bfloat16 [128, 256, 3072], P(('expert', 'group'), 'seq')
Inputs may be any that keep to these rules, and one draw needn't show every extreme that they name: `lengths`: the largest value is 256. `order`: each group number appears once.
All inputs are finite; a program needn't handle non-finite values.
Results may differ from a plain program's by a relative error of at most 0.01.
The roundings to bfloat16 on the way count: a program that leaves them out, or rounds other values in their place, can miss the bound.
Values may be sent and summed in bfloat16 or wider, within the bound.
A program may use at most 256 MiB of HBM per device.

v0:
```python
import jax
import jax.numpy as jnp
from jax import lax
from jax.sharding import PartitionSpec as P

HD = 128


def modulate(embedded, coeffs):
    mean = jnp.mean(embedded, axis=1, keepdims=True)
    centred = embedded - mean
    var = jnp.mean(centred * centred, axis=1, keepdims=True)
    return (centred / jnp.sqrt(var + 1e-06) * (1.0 + coeffs[1]) + coeffs[0]).astype(jnp.bfloat16)


def per_device(
    latents, timestep, boundary, order, lengths, embed_weight, mod_table, qkv_weight, qk_gain
):
    group_index = lax.axis_index("group")
    expert_index = lax.axis_index("expert")
    seq_count = lax.axis_size("seq")
    requests = order.shape[0]
    counter = jnp.arange(requests, dtype=jnp.int32)
    chosen = jnp.sum(jnp.where(order == group_index, counter, 0))
    stamp = lax.dynamic_index_in_dim(timestep, chosen, 0, keepdims=False)
    live_count = lax.dynamic_index_in_dim(lengths, chosen, 0, keepdims=False)
    expert_of = jnp.where(stamp >= boundary[0], 0, 1).astype(jnp.int32)
    active = expert_of == expert_index
    arrived = lax.all_gather(latents, "group", axis=0, tiled=True)
    mine = lax.dynamic_index_in_dim(arrived, chosen, 0, keepdims=False)
    table = mod_table[0]
    steps_all = table.shape[0]
    hit = (jnp.arange(steps_all, dtype=jnp.int32)[None, :] == timestep[:, None]).astype(jnp.float32)
    partial_rows = jnp.einsum("qr,rcd->qcd", hit, table, precision=lax.Precision.HIGHEST)
    all_coeffs = lax.all_gather(partial_rows, ("group", "seq"), axis=2, tiled=True)
    coeffs = lax.dynamic_index_in_dim(all_coeffs, chosen, 0, keepdims=False)
    embed_local = embed_weight[0]
    own = modulate(jnp.dot(mine.T, embed_local, preferred_element_type=jnp.float32), coeffs)
    normed = lax.all_gather(own, "seq", axis=0, tiled=True)
    length_all = normed.shape[0]
    weight_local = qkv_weight[0]
    width = weight_local.shape[2]
    flat = weight_local.reshape(weight_local.shape[0], 3 * width)
    projected = jnp.dot(normed, flat, preferred_element_type=jnp.float32)
    query = projected[:, :width]
    key = projected[:, width : 2 * width]
    value = projected[:, 2 * width :].astype(jnp.bfloat16)
    query_sq, key_sq = lax.psum((jnp.sum(query * query, axis=1), jnp.sum(key * key, axis=1)), "seq")
    features = float(width * seq_count)
    gains = qk_gain[0]
    query_n = (query / jnp.sqrt(query_sq / features + 1e-06)[:, None] * gains[0]).astype(
        jnp.bfloat16
    )
    key_n = (key / jnp.sqrt(key_sq / features + 1e-06)[:, None] * gains[1]).astype(jnp.bfloat16)
    heads_dev = width // HD
    block = min(512, length_all)
    blocks = length_all // block
    keys3 = key_n.reshape(length_all, heads_dev, HD)
    values3 = value.reshape(length_all, heads_dev, HD)
    positions = jnp.arange(length_all, dtype=jnp.int32)
    live_keys = positions < live_count
    query_blocks = query_n.reshape(blocks, block, heads_dev, HD)
    block_starts = jnp.arange(blocks, dtype=jnp.int32) * block

    def attend(operands):
        query_block, start = operands
        scores = jnp.einsum(
            "qhd,khd->hqk", query_block, keys3, preferred_element_type=jnp.float32
        ) * HD ** (-0.5)
        scores = jnp.where(live_keys[None, None, :], scores, -jnp.inf)
        top = jnp.max(scores, axis=2, keepdims=True)
        expd = jnp.exp(scores - top)
        probs = (expd / jnp.sum(expd, axis=2, keepdims=True)).astype(jnp.bfloat16)
        mixed = jnp.einsum("hqk,khd->qhd", probs, values3, preferred_element_type=jnp.float32)
        rows_live = start + jnp.arange(block, dtype=jnp.int32) < live_count
        mixed = jnp.where(rows_live[:, None, None], mixed, 0.0)
        return mixed.reshape(block, width).astype(jnp.bfloat16)

    outputs = lax.map(attend, (query_blocks, block_starts)).reshape(length_all, width)
    returned = lax.all_to_all(outputs, "seq", split_axis=0, concat_axis=1, tiled=True)
    final = jnp.where(active, returned, jnp.zeros_like(returned))
    return final[None]


def solution(mesh):
    in_specs = (
        P("group", None, "seq"),
        P(),
        P(),
        P(),
        P(),
        P("expert", None, None),
        P("expert", None, None, ("group", "seq")),
        P("expert", None, None, "seq"),
        P("expert", None, "seq"),
    )
    out_specs = P(("expert", "group"), "seq", None)
    return jax.shard_map(
        per_device, mesh=mesh, in_specs=in_specs, out_specs=out_specs, check_vma=False
    )
```

profile of v0, /device:TPU:1, one launch (start us, length us, event | category | flops | bytes accessed | tf_op | source)
XLA Modules:
  0.0 378.0 jit_solution(3257790867195534578)
XLA Ops:
  6.5 0.0 copy-start
  6.5 0.0 all-gather.4.cloned.1.call-start
  6.5 0.7 all-gather.4.cloned.1.call-update
  7.3 0.0 all-gather.6.cloned.1.call-start
  7.3 2.0 fusion.10
  9.3 0.0 all-gather.6.cloned.1.call-update
  9.3 0.0 all-gather.8.cloned.1.call-start
  9.4 1.3 fusion.17
  12.4 112.3 %all-gather.4.cloned.1.call-done = bf16[64,64,128]{2,1,0:T(8,128)(2,1)} async-done(((bf16[1,64,128]{2,1,0:T(8,128)(2,1)}), bf16[64,64,128]{2,1,0:T(8,128)(2,1)}) %all-gather.4.cloned.1.call-update) | async-done | bytes 1048592 | tf_op jit(solution)/shard_map/all_gather | solution.py:29
  124.6 0.0 copy-done
  124.6 1.3 fusion.20
  126.0 0.4 multiply_reduce_fusion
  126.4 118.2 %all-gather.6.cloned.1.call-done = f32[64,2,5120]{0,2,1:T(8,128)} async-done(((f32[64,2,40]{0,2,1:T(8,128)}), f32[64,2,5120]{0,2,1:T(8,128)}) %all-gather.6.cloned.1.call-update) | async-done | bytes 2621456 | tf_op jit(solution)/shard_map/all_gather | solution.py:35
  244.6 5.3 %fusion.1 = (f32[5120]{0:T(1024)S(1)}, f32[5120]{0:T(1024)S(1)}) fusion(f32[64,2,5120]{0,2,1:T(8,128)} %all-gather.6.cloned.1.call-done, s32[]{:T(128)S(6)} %select_n.53, s32[]{:T(128)S(6)} %add.75), kind=kLoop, calls=%fused_computation.6 | loop fusion | flops 5120 | bytes 81928 | tf_op jit(solution)/shard_map/add | solution.py:13
  249.9 1.6 add_convert_fusion
  251.5 0.0 all-gather.8.cloned.1.call-update
  251.6 0.0 copy-start.5
  251.6 0.0 copy-start.3
  251.6 61.0 %copy.23 = bf16[1,5120,3,1536]{1,3,2,0:T(8,128)(2,1)} copy(bf16[1,5120,3,1536]{3,1,2,0:T(8,128)(2,1)} %param.16) | data formatting | bytes 94371840 | tf_op args[7]
  312.5 0.0 copy-done.5
  312.5 0.6 dynamic_slice.22
  313.1 0.6 iota_compare_fusion.2
  313.8 0.0 copy-done.3
  313.8 0.0 all-gather.8.cloned.1.call-done
  313.9 22.2 %fusion.22 = f32[256,4608]{1,0:T(8,128)} fusion(bf16[256,5120]{1,0:T(8,128)(2,1)} %all-gather.8.cloned.1.call-done, bf16[5120,4608]{0,1:T(8,128)(2,1)} %bitcast.35), kind=kOutput, calls=%fused_computation.44 | convolution fusion | flops 12079595520 | bytes 54525952 | tf_op jit(solution)/shard_map/dot_general | solution.py:44
  336.1 2.2 multiply_reduce_fusion.1
  338.2 1.5 slice.43
  339.7 3.8 %all-reduce = (f32[256]{0:T(256)S(1)}, f32[256]{0:T(256)S(1)}) all-reduce(f32[256]{0:T(256)S(1)} %get-tuple-element.20, f32[256]{0:T(256)S(1)} %get-tuple-element.19), channel_id=1, replica_groups=mesh['expert'=2,'group'=64,'seq'=2] {'seq'}, use_global_device_ids=true, to_apply=%region_4.5 | all-reduce | flops 512 | bytes 4096 | tf_op jit(solution)/shard_map/psum | solution.py:48
  343.5 2.4 multiply_convert_fusion
  345.9 1.2 copy.26
  347.1 0.0 copy-start.2
  347.1 1.2 copy.25
  348.2 0.3 copy.24
  348.5 0.0 copy-done.2
  348.5 4.0 %fusion.21 = (f32[12,256]{1,0:T(8,128)S(1)}, f32[12,256,256]{1,2,0:T(8,128)}) fusion(pred[256]{0:T(512)(128)(4,1)S(1)} %iota_compare_fusion.2, bf16[256,12,128]{0,2,1:T(8,128)(2,1)} %bitcast.39, bf16[256,12,128]{0,2,1:T(8,128)(2,1)S(1)} %bitcast.37), kind=kOutput, calls=%fused_computation.43 | convolution fusion | flops 204472576 | bytes 4731136 | tf_op jit(solution)/shard_map/while/body/eval_jaxpr/sub | solution.py:72
  352.5 2.3 fusion.7
  354.8 0.0 copy-start.4
  354.8 0.2 convert_element_type.33
  355.0 0.0 copy-start.1
  355.0 1.0 copy.30
  356.0 3.5 all-to-all-start
  359.5 0.0 copy-done.4
  359.6 0.7 dynamic_slice.21
  361.6 8.7 %all-to-all-done = bf16[2,128,1536]{1,2,0:T(8,128)(2,1)S(1)} async-done(((bf16[2,128,1536]{1,2,0:T(8,128)(2,1)}), bf16[2,128,1536]{1,2,0:T(8,128)(2,1)S(1)}, u32[]{:S(2)}, u32[]{:S(2)}) %all-to-all-start) | async-done | bytes 786464 | tf_op jit(solution)/shard_map/all_to_all | solution.py:80
  370.3 0.1 broadcast_select_fusion
  370.3 1.2 copy.31
  371.5 0.0 copy-done.1
  (4 shorter events, 0.1 us)
Async XLA Ops:
  6.5 118.1 %copy-start = (bf16[1,64,5120]{2,1,0:T(8,128)(2,1)S(1)}, bf16[1,64,5120]{2,1,0:T(8,128)(2,1)}, u32[]{:S(2)}) copy-start(bf16[1,64,5120]{2,1,0:T(8,128)(2,1)} %param.14) | copy-start | bytes 1966084
  6.5 118.1 %all-gather.4.cloned.1.call-start = ((), (), s32[]{:S(2)}) async-start(), calls=%async_computation.1 | async-start | bytes 1064960 | tf_op jit(solution)/shard_map/all_gather | solution.py:29
  7.3 237.3 %all-gather.6.cloned.1.call-start = ((), (), s32[]{:S(2)}) async-start(), calls=%async_computation.2 | async-start | bytes 5283840 | tf_op jit(solution)/shard_map/all_gather | solution.py:35
  9.3 304.6 %all-gather.8.cloned.1.call-start = ((), (), s32[]{:S(2)}) async-start(), calls=%async_computation.3 | async-start | bytes 3932160 | tf_op jit(solution)/shard_map/all_gather | solution.py:39
  251.6 61.0 %copy-start.5 = (s32[64]{0:T(128)S(1)}, s32[64]{0:T(128)}, u32[]{:S(2)}) copy-start(s32[64]{0:T(128)} %param.13) | copy-start | bytes 772
  251.6 62.2 %copy-start.3 = (f32[1,2,1536]{2,1,0:T(2,128)S(1)}, f32[1,2,1536]{2,1,0:T(2,128)}, u32[]{:S(2)}) copy-start(f32[1,2,1536]{2,1,0:T(2,128)} %param.17) | copy-start | bytes 36868
  347.1 1.4 copy-start.2
  354.8 4.7 %copy-start.4 = (s32[64]{0:T(128)S(1)}, s32[64]{0:T(128)}, u32[]{:S(2)}) copy-start(s32[64]{0:T(128)} %param.10) | copy-start | bytes 772
  355.0 16.5 %copy-start.1 = (bf16[1,64,5120]{2,1,0:T(8,128)(2,1)S(1)}, bf16[1,64,5120]{2,1,0:T(8,128)(2,1)}, u32[]{:S(2)}) copy-start(bf16[1,64,5120]{2,1,0:T(8,128)(2,1)} %param.14) | copy-start | bytes 1966084
  356.0 14.3 %all-to-all-start = ((bf16[2,128,1536]{1,2,0:T(8,128)(2,1)}), bf16[2,128,1536]{1,2,0:T(8,128)(2,1)S(1)}, u32[]{:S(2)}, u32[]{:S(2)}) async-start(bf16[2,128,1536]{1,2,0:T(8,128)(2,1)} %copy.30), calls=%async_computation | async-start | bytes 1572864 | tf_op jit(solution)/shard_map/all_to_all | solution.py:80
Sparse Core Ops, SparseCore 0:
  11.0 113.6 all-gather.3
  128.1 116.4 all-gather.5
  251.7 44.5 all-gather.7
where the time goes:
time: 380 us; the launch traced here: 378 us
  waiting for transfers between devices  240 us (63%)
  local copies, waits for them, and re-layouts  68.7 us (18%)
  matrix products  31.8 us (8%)
  between operations  16.3 us (4%)
  other arithmetic  13.9 us (4%)
    all_gather x1, waiting for transfers between devices, per_device(): lax.all_gather(partial_rows, ('group', 'seq'), axis=2, tiled=True)  118 us
    all_gather x1, waiting for transfers between devices, per_device(): arrived = lax.all_gather(latents, 'group', axis=0, tiled=True)  112 us
    unnamed x13, local copies, waits for them, and re-layouts  61 us
    dot_general x1, matrix products, per_device(): projected = jnp.dot(normed, flat, preferred_element_type=jnp.float32)  22.2 us
    all_to_all x1, waiting for transfers between devices, per_device(): lax.all_to_all(outputs, 'seq', split_axis=0, concat_axis=1, tiled=True)  8.68 us
  transfers between devices with their start and end apart: 4, of which 3 were waited for; matrix products, arithmetic and copies ran while one was open for 18% of the time, Pallas kernels for 0%

commit v1 on v0

v1 whole, which is shorter than its diff:
```python
import jax
import jax.numpy as jnp
from jax import lax
from jax.experimental import pallas as pl
from jax.experimental.pallas import tpu as pltpu
from jax.sharding import PartitionSpec as P

HD = 128
EPS = 1e-06
MESH = pl.DeviceIdType.MESH
F32 = jnp.float32
BF16 = jnp.bfloat16
NZ = 8
ND = 8
CW = 256
HI = lax.Precision.HIGHEST


def kernel(
    order_s, time_s, bound_s, len_s, lat_ref, gain_ref, emb_hbm, tab_hbm, w_hbm,
    out_hbm,
    emb_v, tab_v, wbuf,
    lat_all, lat_send, lat_recv, mod_src, mod_all, mod_send, mod_recv, mod_row,
    xt, normed, proj, vbuf, kbuf, sq_send, sq_recv, out_far, out_own,
    loc_sem, w_sem, l1_send, l1_recv, m1_send, m1_recv, l2_send, l2_recv, m2_send, m2_recv,
    sq_sem, o_send, o_recv,
):
    g = lax.axis_index("group")
    s = lax.axis_index("seq")
    e = lax.axis_index("expert")
    z = g // ND
    d = g % ND
    p = d * 2 + s
    reqs = NZ * ND
    tokens = 256
    half = 128
    feats = emb_v.shape[1]
    chunks = w_hbm.shape[2] // CW
    width = w_hbm.shape[2]

    emb_cp = pltpu.make_async_copy(emb_hbm.at[0], emb_v, loc_sem.at[0])
    tab_cp = pltpu.make_async_copy(tab_hbm, tab_v, loc_sem.at[1])
    tab_cp.start()
    emb_cp.start()

    def w_copy(i):
        return pltpu.make_async_copy(
            w_hbm.at[i // chunks, :, pl.ds(pl.multiple_of((i % chunks) * CW, CW), CW)],
            wbuf.at[i], w_sem.at[i],
        )

    barrier = pltpu.get_barrier_semaphore()

    def greet_z(k, c):
        pl.semaphore_signal(barrier, inc=1, device_id={"group": ((z + k) % NZ) * ND + d}, device_id_type=MESH)
        return c

    def greet_p(k, c):
        q = (p + k) % (2 * ND)
        pl.semaphore_signal(barrier, inc=1, device_id={"group": z * ND + q // 2, "seq": q % 2}, device_id_type=MESH)
        return c

    lax.fori_loop(1, NZ, greet_z, 0)
    lax.fori_loop(1, 2 * ND, greet_p, 0)
    pl.semaphore_wait(barrier, NZ - 1 + 2 * ND - 1)

    def l1_copy(k, slot):
        return pltpu.make_async_remote_copy(
            src_ref=lat_ref.at[0], dst_ref=lat_all.at[slot], send_sem=l1_send.at[k], recv_sem=l1_recv.at[slot],
            device_id={"group": ((z + k) % NZ) * ND + d}, device_id_type=MESH)

    def l1_start(k, c):
        l1_copy(k, z).start()
        return c

    lax.fori_loop(1, NZ, l1_start, 0)
    lat_all[z] = lat_ref[0]

    def w_start(i, c):
        w_copy(i).start()
        return c

    lax.fori_loop(0, 3 * chunks, w_start, 0)

    rows = lax.broadcasted_iota(jnp.int32, (reqs, 128), 0)

    def pick(r, c):
        col, stamp, live = c
        where = order_s[r]
        col = jnp.where(rows == where, time_s[r], col)
        mine = where == g
        return col, jnp.where(mine, time_s[r], stamp), jnp.where(mine, len_s[r], live)

    col, stamp, live = lax.fori_loop(
        0, reqs, pick, (jnp.zeros((reqs, 128), jnp.int32), jnp.int32(0), jnp.int32(0)), unroll=8)
    expert_of = jnp.where(stamp >= bound_s[0], 0, 1)
    shown = jnp.where(expert_of == e, live, 0)

    steps = tab_v.shape[1]
    tab_cp.wait()
    hit = (lax.broadcasted_iota(jnp.int32, (reqs, steps), 1) == col[:, :1]).astype(F32)
    picked = lax.dot_general(hit, tab_v[...], (((1,), (1,)), ((), ())), precision=HI, preferred_element_type=F32)
    mod_src[...] = jnp.zeros_like(mod_src)
    for a in range(NZ):
        mod_src[a, :, : tab_v.shape[0]] = picked[a * ND : (a + 1) * ND]

    def m1_copy(k, slot):
        z2 = (z + k) % NZ
        return pltpu.make_async_remote_copy(
            src_ref=mod_src.at[z2], dst_ref=mod_all.at[slot], send_sem=m1_send.at[k], recv_sem=m1_recv.at[slot],
            device_id={"group": z2 * ND + d}, device_id_type=MESH)

    def m1_start(k, c):
        m1_copy(k, z).start()
        return c

    lax.fori_loop(1, NZ, m1_start, 0)
    mod_all[z] = mod_src[z]

    def l1_wait(k, c):
        l1_copy(k, (z + k) % NZ).wait_recv()
        return c

    lax.fori_loop(1, NZ, l1_wait, 0)
    for b in range(ND):
        chosen = jnp.zeros(lat_all.shape[1:], BF16)
        for a in range(NZ):
            chosen = jnp.where(order_s[a * ND + d] == z * ND + b, lat_all[a], chosen)
        lat_send[b] = chosen

    def l2_copy(k, slot):
        q = (p + k) % (2 * ND)
        return pltpu.make_async_remote_copy(
            src_ref=lat_send.at[q // 2], dst_ref=lat_recv.at[slot], send_sem=l2_send.at[k], recv_sem=l2_recv.at[slot],
            device_id={"group": z * ND + q // 2, "seq": q % 2}, device_id_type=MESH)

    def l2_start(k, c):
        l2_copy(k, p).start()
        return c

    lax.fori_loop(1, 2 * ND, l2_start, 0)
    lat_recv[p] = lat_send[d]

    def m1_wait(k, c):
        m1_copy(k, (z + k) % NZ).wait_recv()
        return c

    lax.fori_loop(1, NZ, m1_wait, 0)
    for b in range(ND):
        for a in range(NZ):
            mod_send[b, a : a + 1] = mod_all[a, b : b + 1]

    def m2_copy(k, slot):
        q = (p + k) % (2 * ND)
        return pltpu.make_async_remote_copy(
            src_ref=mod_send.at[q // 2], dst_ref=mod_recv.at[slot], send_sem=m2_send.at[k], recv_sem=m2_recv.at[slot],
            device_id={"group": z * ND + q // 2, "seq": q % 2}, device_id_type=MESH)

    def m2_start(k, c):
        m2_copy(k, p).start()
        return c

    lax.fori_loop(1, 2 * ND, m2_start, 0)
    mod_recv[p] = mod_send[d]

    emb_cp.wait()
    wbar = jnp.sum(emb_v[...].astype(F32), axis=1, keepdims=True) * (1.0 / feats)
    wbar = jnp.broadcast_to(wbar, (wbar.shape[0], 128))

    def l2_wait(k, c):
        l2_copy(k, (p + k) % (2 * ND)).wait_recv()
        return c

    lax.fori_loop(1, 2 * ND, l2_wait, 0)
    for t in range(2):
        x = lat_recv[t].astype(F32)
        for b in range(1, ND):
            x = x + lat_recv[2 * b + t].astype(F32)
        xt[t * half : (t + 1) * half] = jnp.transpose(x).astype(BF16)

    mean = lax.dot_general(xt[...].astype(F32), wbar, (((1,), (0,)), ((), ())), precision=HI, preferred_element_type=F32)
    et = 256
    tiles = feats // et

    def embed(t, i):
        cols = pl.ds(pl.multiple_of(i * et, et), et)
        made = jnp.dot(xt[t * half : (t + 1) * half], emb_v[:, cols], preferred_element_type=F32)
        m = mean[t * half : (t + 1) * half, :1]
        return made - m

    def spread(t):
        def body(i, ss):
            c = embed(t, i)
            c = c * c
            return ss + c[:, :128] + c[:, 128:]
        ss = lax.fori_loop(0, tiles, body, jnp.zeros((half, 128), F32))
        var = jnp.sum(ss, axis=1, keepdims=True) * (1.0 / feats)
        return 1.0 / jnp.sqrt(var + EPS)

    rstd = [spread(t) for t in range(2)]

    def m2_wait(k, c):
        m2_copy(k, (p + k) % (2 * ND)).wait_recv()
        return c

    lax.fori_loop(1, 2 * ND, m2_wait, 0)
    own = tab_v.shape[0] // 2
    lane = lax.broadcasted_iota(jnp.int32, (NZ, 128), 1)
    span = 2 * ND * own // 128
    for c in range(2):
        pieces = [jnp.zeros((NZ, 128), F32) for _ in range(span)]
        for q in range(2 * ND):
            start = q * own
            off = start % 128
            turned = pltpu.roll(mod_recv[q], (off - c * own) % 128, 1)
            a = start // 128
            pieces[a] = jnp.where((lane >= off) & (lane < off + own), turned, pieces[a])
            if off + own > 128:
                pieces[a + 1] = jnp.where(lane < off + own - 128, turned, pieces[a + 1])
        for a in range(span):
            for b in range(NZ):
                n = (b * span + a) * 128
                mod_row[c : c + 1, n : n + 128] = pieces[a][b : b + 1] + float(c)

    for t in range(2):
        def body(i, c, t=t):
            cols = pl.ds(pl.multiple_of(i * et, et), et)
            v = embed(t, i) * rstd[t] * mod_row[1:2, cols] + mod_row[0:1, cols]
            normed[t * half : (t + 1) * half, cols] = v.astype(BF16)
            return c
        lax.fori_loop(0, tiles, body, 0)

    def project(i):
        w_copy(i).wait()
        return jnp.dot(normed[...], wbuf[i], preferred_element_type=F32)

    def squares(base):
        def body(i, ss):
            made = project(base + i)
            proj[base + i] = made
            made = made * made
            return ss + made[:, :128] + made[:, 128:]
        ss = lax.fori_loop(0, chunks, body, jnp.zeros((tokens, 128), F32))
        return jnp.sum(ss, axis=1, keepdims=True)

    q_ss = squares(0)
    k_ss = squares(chunks)
    lane_t = lax.broadcasted_iota(jnp.int32, (tokens, 128), 1)
    sq_send[...] = jnp.where(lane_t < 64, q_ss, k_ss)
    sq_cp = pltpu.make_async_remote_copy(
        src_ref=sq_send, dst_ref=sq_recv, send_sem=sq_sem.at[0], recv_sem=sq_sem.at[1],
        device_id={"seq": 1 - s}, device_id_type=MESH)
    sq_cp.start()

    def values(i, c):
        vbuf[i] = project(2 * chunks + i).astype(BF16)
        return c

    lax.fori_loop(0, chunks, values, 0)
    sq_cp.wait_recv()
    total = sq_send[...] + sq_recv[...]
    inv = 1.0 / jnp.sqrt(total * (1.0 / (2 * width)) + EPS)
    sq_send_done = sq_cp.wait_send
    sq_send_done()
    sq_send[...] = inv

    keypos = lax.broadcasted_iota(jnp.int32, (half, tokens), 1)
    rowpos = lax.broadcasted_iota(jnp.int32, (half, HD), 0)

    def attend(i, r0, out_ref, first):
        cols = pl.ds(pl.multiple_of(i * CW, CW), CW)
        gq = gain_ref[0, 0:1, cols]
        at = pl.ds(pl.multiple_of(r0, half), half)
        if first:
            gk = gain_ref[0, 1:2, cols]
            kbuf[i] = (proj[chunks + i] * sq_send[:, 64:65] * gk).astype(BF16)
        q2 = (proj[i, at, :] * sq_send[at, 0:1] * gq).astype(BF16)
        for j in range(CW // HD):
            hc = slice(j * HD, (j + 1) * HD)
            sc = lax.dot_general(q2[:, hc], kbuf[i, :, hc], (((1,), (1,)), ((), ())), preferred_element_type=F32)
            sc = jnp.where(keypos < live, sc * HD ** (-0.5), -jnp.inf)
            ex = jnp.exp(sc - jnp.max(sc, axis=1, keepdims=True))
            pr = (ex * (1.0 / jnp.sum(ex, axis=1, keepdims=True))).astype(BF16)
            mixed = jnp.dot(pr, vbuf[i, :, hc], preferred_element_type=F32)
            mixed = jnp.where(rowpos + r0 < shown, mixed, 0.0)
            out_ref[:, pl.ds(pl.multiple_of(i * CW + j * HD, HD), HD)] = mixed.astype(BF16)

    def o_copy(i, side):
        cols = pl.ds(pl.multiple_of(i * CW, CW), CW)
        there = pl.ds(pl.multiple_of(side * width + i * CW, CW), CW)
        return pltpu.make_async_remote_copy(
            src_ref=out_far.at[:, cols], dst_ref=out_hbm.at[0, :, there], send_sem=o_send.at[i], recv_sem=o_recv.at[i],
            device_id={"seq": 1 - s}, device_id_type=MESH)

    def far(i, c):
        attend(i, (1 - s) * half, out_far, True)
        o_copy(i, s).start()
        return c

    lax.fori_loop(0, chunks, far, 0)

    def near(i, c):
        attend(i, s * half, out_own, False)
        return c

    lax.fori_loop(0, chunks, near, 0)
    own_cp = pltpu.make_async_copy(
        out_own, out_hbm.at[0, :, pl.ds(pl.multiple_of(s * width, width), width)], loc_sem.at[2])
    own_cp.start()

    def sends_z(k, c):
        l1_copy(k, z).wait_send()
        m1_copy(k, z).wait_send()
        return c

    def sends_p(k, c):
        l2_copy(k, p).wait_send()
        m2_copy(k, p).wait_send()
        return c

    lax.fori_loop(1, NZ, sends_z, 0)
    lax.fori_loop(1, 2 * ND, sends_p, 0)

    def o_wait(i, c):
        o_copy(i, 1 - s).wait_recv()
        o_copy(i, s).wait_send()
        return c

    lax.fori_loop(0, chunks, o_wait, 0)
    own_cp.wait()


def per_device(latents, timestep, boundary, order, lengths, embed_weight, mod_table, qkv_weight, qk_gain):
    patch, feats = embed_weight.shape[1:]
    width = qkv_weight.shape[3]
    chunks = width // CW
    steps = mod_table.shape[1]
    table = jnp.transpose(mod_table[0], (1, 2, 0)).reshape(-1, steps)
    weights = jnp.transpose(qkv_weight[0], (1, 0, 2))
    tokens, half = 256, 128
    smem = pl.BlockSpec(memory_space=pltpu.SMEM)
    vmem = pl.BlockSpec(memory_space=pltpu.VMEM)
    anywhere = pl.BlockSpec(memory_space=pl.ANY)
    dma = pltpu.SemaphoreType.DMA
    return pl.pallas_call(
        kernel,
        out_shape=jax.ShapeDtypeStruct((1, half, 2 * width), BF16),
        in_specs=[smem] * 4 + [vmem] * 2 + [anywhere] * 3,
        out_specs=anywhere,
        scratch_shapes=[
            pltpu.VMEM((patch, feats), BF16),
            pltpu.VMEM(table.shape, F32),
            pltpu.VMEM((3 * chunks, feats, CW), BF16),
            pltpu.VMEM((NZ, patch, half), BF16),
            pltpu.VMEM((ND, patch, half), BF16),
            pltpu.VMEM((2 * ND, patch, half), BF16),
            pltpu.VMEM((NZ, ND, 128), F32),
            pltpu.VMEM((NZ, ND, 128), F32),
            pltpu.VMEM((ND, NZ, 128), F32),
            pltpu.VMEM((2 * ND, NZ, 128), F32),
            pltpu.VMEM((2, feats), F32),
            pltpu.VMEM((tokens, patch), BF16),
            pltpu.VMEM((tokens, feats), BF16),
            pltpu.VMEM((2 * chunks, tokens, CW), F32),
            pltpu.VMEM((chunks, tokens, CW), BF16),
            pltpu.VMEM((chunks, tokens, CW), BF16),
            pltpu.VMEM((tokens, 128), F32),
            pltpu.VMEM((tokens, 128), F32),
            pltpu.VMEM((half, width), BF16),
            pltpu.VMEM((half, width), BF16),
            dma((3,)),
            dma((3 * chunks,)),
            dma((NZ,)), dma((NZ,)), dma((NZ,)), dma((NZ,)),
            dma((2 * ND,)), dma((2 * ND,)), dma((2 * ND,)), dma((2 * ND,)),
            dma((2,)),
            dma((chunks,)), dma((chunks,)),
        ],
        compiler_params=pltpu.CompilerParams(
            collective_id=0, has_side_effects=True, vmem_limit_bytes=62 * 1024 * 1024),
        cost_estimate=pl.CostEstimate(flops=13 * 10**9, bytes_accessed=49 * 10**6, transcendentals=800000),
    )(order, timestep, boundary, lengths, latents, qk_gain, embed_weight, table, weights)


def solution(mesh):
    in_specs = (
        P("group", None, "seq"),
        P(),
        P(),
        P(),
        P(),
        P("expert", None, None),
        P("expert", None, None, ("group", "seq")),
        P("expert", None, None, "seq"),
        P("expert", None, "seq"),
    )
    out_specs = P(("expert", "group"), "seq", None)
    return jax.shard_map(
        per_device, mesh=mesh, in_specs=in_specs, out_specs=out_specs, check_vma=False
    )
```

time: 380 us -> 65.1 us (0.17)
  waiting for transfers between devices: 240 us -> 0 us
  local copies, waits for them, and re-layouts: 68.7 us -> 2.06 us
  Pallas kernels: 0 us -> 61.7 us
  matrix products: 31.8 us -> 0 us
  between operations: 16.3 us -> 0.66 us
  other arithmetic: 13.9 us -> 0 us
    all_gather x3 -> x0, waiting for transfers between devices: 230 us -> none  [the longest x1 118 us: per_device(): lax.all_gather(partial_rows, ('group', 'seq'), axis=2, tiled=True)]
    pallas_call x0 -> x1, Pallas kernels: none -> 61.7 us  [per_device(): pl.pallas_call(kernel, out_shape=jax.ShapeDtypeStruct((1, half, 2 * width...]
    unnamed x13 -> x1, local copies, waits for them, and re-layouts: 61 us -> 2.06 us
    dot_general x3 -> x0, matrix products: 25.8 us -> none  [the longest x1 22.2 us: per_device(): projected = jnp.dot(normed, flat, preferred_element_type=jnp.float32)]
    all_to_all x1 -> x0, waiting for transfers between devices: 8.68 us -> none  [per_device(): lax.all_to_all(outputs, 'seq', split_axis=0, concat_axis=1, tiled=True)]
    add x1 -> x0, other arithmetic: 5.32 us -> none  [modulate(): 1.0 + coeffs[1]]
    sub x1 -> x0, matrix products: 4 us -> none  [attend(): expd = jnp.exp(scores - top)]
    convert_element_type x2 -> x0, other arithmetic: 4 us -> none  [the longest x1 2.39 us: per_device(): (key / jnp.sqrt(key_sq / features + 1e-06)[:, None] * gains[1]).astype(jn...]
  transfers between devices with their start and end apart: 4 -> 0, of which waited for: 3 -> 0; matrix products, arithmetic and copies ran while one was open for 18% -> 0% of each run, Pallas kernels for 0% -> 0%
where the time goes in v1:
time: 65.1 us; the launch traced here: 64.4 us
  Pallas kernels  61.7 us (95%)
  local copies, waits for them, and re-layouts  2.06 us (3%)
  between operations  0.66 us (1%)
    pallas_call x1, Pallas kernels, per_device(): pl.pallas_call(kernel, out_shape=jax.ShapeDtypeStruct((1, half, 2 * width...  61.7 us
    unnamed x1, local copies, waits for them, and re-layouts  2.06 us

profile of v1, /device:TPU:1, one launch (start us, length us, event | category | flops | bytes accessed | tf_op | source)
XLA Modules:
  0.0 64.4 jit_solution(12874586457662342713)
XLA Ops:
  0.7 61.7 %shard_map.91 = bf16[1,128,3072]{2,1,0:T(8,128)(2,1)} custom-call(s32[64]{0:T(128)} %order_s.1, s32[64]{0:T(128)} %time_s.1, s32[1]{0:T(128)S(6)} %copy.11.bound_s, s32[64]{0:T(128)} %len_s.1, bf16[1,64,128]{2,1,0:T(8,128)(2,1)} %lat_ref.1, f32[1,2,1536]{2,1,0:T(2,128)} %gain_ref.1, bf16[1,64,5120]{2,1,0:T(8,128)(2,1)} %emb_hbm.1, f32[80,1024]{1,0:T(8,128)} %bitcast.9, ...), custom_call_target="tpu_custom_call" | custom-call | flops 12999999488 | bytes 49000000 | tf_op jit(solution)/shard_map/pallas_call | solution.py:345
  62.4 2.1 %copy.12 = bf16[1,128,3072]{2,1,0:T(8,128)(2,1)} copy(bf16[1,128,3072]{2,1,0:T(8,128)(2,1)} %shard_map.91) | data formatting | bytes 1572864

commit v2 on v1

--- a/solution.py
+++ b/solution.py
@@ -14,6 +14,8 @@
 ND = 8
 CW = 256
 HI = lax.Precision.HIGHEST
+UNROLL = 3
+PAIRS = 3
 
 
 def kernel(
@@ -21,7 +23,7 @@
     out_hbm,
     emb_v, tab_v, wbuf,
     lat_all, lat_send, lat_recv, mod_src, mod_all, mod_send, mod_recv, mod_row,
-    xt, normed, proj, vbuf, kbuf, sq_send, sq_recv, out_far, out_own,
+    xt, normed, proj, vbuf, kbuf, sq_send, sq_recv, inv_qk, out_far, out_own,
     loc_sem, w_sem, l1_send, l1_recv, m1_send, m1_recv, l2_send, l2_recv, m2_send, m2_recv,
     sq_sem, o_send, o_recv,
 ):
@@ -49,6 +51,12 @@
             wbuf.at[i], w_sem.at[i],
         )
 
+    def w_start(i, c):
+        w_copy(i).start()
+        return c
+
+    lax.fori_loop(0, 3 * chunks, w_start, 0)
+
     barrier = pltpu.get_barrier_semaphore()
 
     def greet_z(k, c):
@@ -75,12 +83,6 @@
 
     lax.fori_loop(1, NZ, l1_start, 0)
     lat_all[z] = lat_ref[0]
-
-    def w_start(i, c):
-        w_copy(i).start()
-        return c
-
-    lax.fori_loop(0, 3 * chunks, w_start, 0)
 
     rows = lax.broadcasted_iota(jnp.int32, (reqs, 128), 0)
 
@@ -181,21 +183,23 @@
     mean = lax.dot_general(xt[...].astype(F32), wbar, (((1,), (0,)), ((), ())), precision=HI, preferred_element_type=F32)
     et = 256
     tiles = feats // et
-
-    def embed(t, i):
-        cols = pl.ds(pl.multiple_of(i * et, et), et)
-        made = jnp.dot(xt[t * half : (t + 1) * half], emb_v[:, cols], preferred_element_type=F32)
-        m = mean[t * half : (t + 1) * half, :1]
-        return made - m
+    near_each = 10
+
+    def embed(t, n):
+        made = jnp.dot(xt[t * half : (t + 1) * half], emb_v[:, pl.ds(pl.multiple_of(n * et, et), et)],
+                       preferred_element_type=F32)
+        m = mean[t * half : (t + 1) * half]
+        return made[:, :128] - m, made[:, 128:] - m
 
     def spread(t):
         def body(i, ss):
-            c = embed(t, i)
-            c = c * c
-            return ss + c[:, :128] + c[:, 128:]
-        ss = lax.fori_loop(0, tiles, body, jnp.zeros((half, 128), F32))
+            for u in range(near_each):
+                c0, c1 = embed(t, i * near_each + u)
+                ss = ss + (c0 * c0 + c1 * c1)
+            return ss
+        ss = lax.fori_loop(0, tiles // near_each, body, jnp.zeros((half, 128), F32))
         var = jnp.sum(ss, axis=1, keepdims=True) * (1.0 / feats)
-        return 1.0 / jnp.sqrt(var + EPS)
+        return jnp.broadcast_to(1.0 / jnp.sqrt(var + EPS), (half, 128))
 
     rstd = [spread(t) for t in range(2)]
 
@@ -224,14 +228,22 @@
 
     for t in range(2):
         def body(i, c, t=t):
-            cols = pl.ds(pl.multiple_of(i * et, et), et)
-            v = embed(t, i) * rstd[t] * mod_row[1:2, cols] + mod_row[0:1, cols]
-            normed[t * half : (t + 1) * half, cols] = v.astype(BF16)
+            for u in range(near_each):
+                n = i * near_each + u
+                for h, v in enumerate(embed(t, n)):
+                    cols = pl.ds(pl.multiple_of(n * et + h * 128, 128), 128)
+                    v = v * rstd[t] * mod_row[1:2, cols] + mod_row[0:1, cols]
+                    normed[t * half : (t + 1) * half, cols] = v.astype(BF16)
             return c
-        lax.fori_loop(0, tiles, body, 0)
+        lax.fori_loop(0, tiles // near_each, body, 0)
+
+    def arrive(base):
+        def body(i, c):
+            w_copy(base + i).wait()
+            return c
+        lax.fori_loop(0, chunks, body, 0)
 
     def project(i):
-        w_copy(i).wait()
         return jnp.dot(normed[...], wbuf[i], preferred_element_type=F32)
 
     def squares(base):
@@ -239,14 +251,20 @@
             made = project(base + i)
             proj[base + i] = made
             made = made * made
-            return ss + made[:, :128] + made[:, 128:]
-        ss = lax.fori_loop(0, chunks, body, jnp.zeros((tokens, 128), F32))
-        return jnp.sum(ss, axis=1, keepdims=True)
-
+            return ss + (made[:, :128] + made[:, 128:])
+        return lax.fori_loop(0, chunks, body, jnp.zeros((tokens, 128), F32), unroll=UNROLL)
+
+    ones = jnp.ones((8, 128), F32)
+
+    def as_rows(ss):
+        return lax.dot_general(ones, ss, (((1,), (1,)), ((), ())), precision=HI, preferred_element_type=F32)
+
+    arrive(0)
     q_ss = squares(0)
+    arrive(chunks)
     k_ss = squares(chunks)
-    lane_t = lax.broadcasted_iota(jnp.int32, (tokens, 128), 1)
-    sq_send[...] = jnp.where(lane_t < 64, q_ss, k_ss)
+    sq_send[0] = as_rows(q_ss)
+    sq_send[1] = as_rows(k_ss)
     sq_cp = pltpu.make_async_remote_copy(
         src_ref=sq_send, dst_ref=sq_recv, send_sem=sq_sem.at[0], recv_sem=sq_sem.at[1],
         device_id={"seq": 1 - s}, device_id_type=MESH)
@@ -256,34 +274,41 @@
         vbuf[i] = project(2 * chunks + i).astype(BF16)
         return c
 
-    lax.fori_loop(0, chunks, values, 0)
+    first = chunks // 2
+    arrive(2 * chunks)
+    lax.fori_loop(0, first, values, 0, unroll=UNROLL)
     sq_cp.wait_recv()
-    total = sq_send[...] + sq_recv[...]
-    inv = 1.0 / jnp.sqrt(total * (1.0 / (2 * width)) + EPS)
-    sq_send_done = sq_cp.wait_send
-    sq_send_done()
-    sq_send[...] = inv
+    for c in range(2):
+        total = sq_send[c] + sq_recv[c]
+        inv = 1.0 / jnp.sqrt(total * (1.0 / (2 * width)) + EPS)
+        inv = jnp.broadcast_to(inv[0:1], (128, tokens))
+        inv_qk[c] = jnp.transpose(inv)
 
     keypos = lax.broadcasted_iota(jnp.int32, (half, tokens), 1)
     rowpos = lax.broadcasted_iota(jnp.int32, (half, HD), 0)
 
     def attend(i, r0, out_ref, first):
-        cols = pl.ds(pl.multiple_of(i * CW, CW), CW)
-        gq = gain_ref[0, 0:1, cols]
         at = pl.ds(pl.multiple_of(r0, half), half)
-        if first:
-            gk = gain_ref[0, 1:2, cols]
-            kbuf[i] = (proj[chunks + i] * sq_send[:, 64:65] * gk).astype(BF16)
-        q2 = (proj[i, at, :] * sq_send[at, 0:1] * gq).astype(BF16)
-        for j in range(CW // HD):
-            hc = slice(j * HD, (j + 1) * HD)
-            sc = lax.dot_general(q2[:, hc], kbuf[i, :, hc], (((1,), (1,)), ((), ())), preferred_element_type=F32)
+        work = []
+        for u in range(PAIRS):
+            n = i * PAIRS + u
+            for j in range(CW // HD):
+                hc = slice(j * HD, (j + 1) * HD)
+                cols = pl.ds(pl.multiple_of(n * CW + j * HD, HD), HD)
+                if first:
+                    kbuf[n, :, hc] = (proj[chunks + n, :, hc] * inv_qk[1] * gain_ref[0, 1:2, cols]).astype(BF16)
+                qn = (proj[n, at, hc] * inv_qk[0, at, :] * gain_ref[0, 0:1, cols]).astype(BF16)
+                work.append((n, hc, cols, qn))
+        scores = [lax.dot_general(qn, kbuf[n, :, hc], (((1,), (1,)), ((), ())), preferred_element_type=F32)
+                  for n, hc, _, qn in work]
+        parts = []
+        for sc in scores:
             sc = jnp.where(keypos < live, sc * HD ** (-0.5), -jnp.inf)
             ex = jnp.exp(sc - jnp.max(sc, axis=1, keepdims=True))
-            pr = (ex * (1.0 / jnp.sum(ex, axis=1, keepdims=True))).astype(BF16)
-            mixed = jnp.dot(pr, vbuf[i, :, hc], preferred_element_type=F32)
-            mixed = jnp.where(rowpos + r0 < shown, mixed, 0.0)
-            out_ref[:, pl.ds(pl.multiple_of(i * CW + j * HD, HD), HD)] = mixed.astype(BF16)
+            parts.append((ex * (1.0 / jnp.sum(ex, axis=1, keepdims=True))).astype(BF16))
+        for (n, hc, cols, _), pr in zip(work, parts):
+            mixed = jnp.dot(pr, vbuf[n, :, hc], preferred_element_type=F32)
+            out_ref[:, cols] = jnp.where(rowpos + r0 < shown, mixed, 0.0).astype(BF16)
 
     def o_copy(i, side):
         cols = pl.ds(pl.multiple_of(i * CW, CW), CW)
@@ -294,16 +319,20 @@
 
     def far(i, c):
         attend(i, (1 - s) * half, out_far, True)
-        o_copy(i, s).start()
-        return c
-
-    lax.fori_loop(0, chunks, far, 0)
+        for u in range(PAIRS):
+            o_copy(i * PAIRS + u, s).start()
+        return c
+
+    far(0, 0)
+    lax.fori_loop(first, chunks, values, 0, unroll=UNROLL)
+    far(1, 0)
 
     def near(i, c):
         attend(i, s * half, out_own, False)
         return c
 
-    lax.fori_loop(0, chunks, near, 0)
+    near(0, 0)
+    near(1, 0)
     own_cp = pltpu.make_async_copy(
         out_own, out_hbm.at[0, :, pl.ds(pl.multiple_of(s * width, width), width)], loc_sem.at[2])
     own_cp.start()
@@ -326,6 +355,7 @@
         o_copy(i, s).wait_send()
         return c
 
+    sq_cp.wait_send()
     lax.fori_loop(0, chunks, o_wait, 0)
     own_cp.wait()
 
@@ -364,8 +394,9 @@
             pltpu.VMEM((2 * chunks, tokens, CW), F32),
             pltpu.VMEM((chunks, tokens, CW), BF16),
             pltpu.VMEM((chunks, tokens, CW), BF16),
-            pltpu.VMEM((tokens, 128), F32),
-            pltpu.VMEM((tokens, 128), F32),
+            pltpu.VMEM((2, 8, tokens), F32),
+            pltpu.VMEM((2, 8, tokens), F32),
+            pltpu.VMEM((2, tokens, 128), F32),
             pltpu.VMEM((half, width), BF16),
             pltpu.VMEM((half, width), BF16),
             dma((3,)),
@@ -376,7 +407,7 @@
             dma((chunks,)), dma((chunks,)),
         ],
         compiler_params=pltpu.CompilerParams(
-            collective_id=0, has_side_effects=True, vmem_limit_bytes=62 * 1024 * 1024),
+            collective_id=0, has_side_effects=True, vmem_limit_bytes=57 * 1024 * 1024),
         cost_estimate=pl.CostEstimate(flops=13 * 10**9, bytes_accessed=49 * 10**6, transcendentals=800000),
     )(order, timestep, boundary, lengths, latents, qk_gain, embed_weight, table, weights)
 

time: 65.1 us -> 51.9 us (0.80)
  Pallas kernels: 61.7 us -> 48.8 us
    pallas_call x1, Pallas kernels: 61.7 us -> 48.8 us  [per_device(): pl.pallas_call(kernel, out_shape=jax.ShapeDtypeStruct((1, half, 2 * width...]
where the time goes in v2:
time: 51.9 us; the launch traced here: 51.5 us
  Pallas kernels  48.8 us (94%)
  local copies, waits for them, and re-layouts  2.06 us (4%)
  between operations  0.66 us (1%)
    pallas_call x1, Pallas kernels, per_device(): pl.pallas_call(kernel, out_shape=jax.ShapeDtypeStruct((1, half, 2 * width...  48.8 us
    unnamed x1, local copies, waits for them, and re-layouts  2.06 us

profile of v2, /device:TPU:1, one launch (start us, length us, event | category | flops | bytes accessed | tf_op | source)
XLA Modules:
  0.0 51.5 jit_solution(11277187800593182575)
XLA Ops:
  0.7 48.8 %shard_map.91 = bf16[1,128,3072]{2,1,0:T(8,128)(2,1)} custom-call(s32[64]{0:T(128)} %order_s.1, s32[64]{0:T(128)} %time_s.1, s32[1]{0:T(128)S(6)} %copy.11.bound_s, s32[64]{0:T(128)} %len_s.1, bf16[1,64,128]{2,1,0:T(8,128)(2,1)} %lat_ref.1, f32[1,2,1536]{2,1,0:T(2,128)} %gain_ref.1, bf16[1,64,5120]{2,1,0:T(8,128)(2,1)} %emb_hbm.1, f32[80,1024]{1,0:T(8,128)} %bitcast.9, ...), custom_call_target="tpu_custom_call" | custom-call | flops 12999999488 | bytes 49000000 | tf_op jit(solution)/shard_map/pallas_call | solution.py:375
  49.5 2.1 %copy.12 = bf16[1,128,3072]{2,1,0:T(8,128)(2,1)} copy(bf16[1,128,3072]{2,1,0:T(8,128)(2,1)} %shard_map.91) | data formatting | bytes 1572864

commit v3 on v2

--- a/solution.py
+++ b/solution.py
@@ -14,7 +14,8 @@
 ND = 8
 CW = 256
 HI = lax.Precision.HIGHEST
-UNROLL = 3
+UNROLL = 6
+NORM = 20
 PAIRS = 3
 
 
@@ -81,7 +82,7 @@
         l1_copy(k, z).start()
         return c
 
-    lax.fori_loop(1, NZ, l1_start, 0)
+    lax.fori_loop(1, NZ, l1_start, 0, unroll=True)
     lat_all[z] = lat_ref[0]
 
     rows = lax.broadcasted_iota(jnp.int32, (reqs, 128), 0)
@@ -100,8 +101,16 @@
 
     steps = tab_v.shape[1]
     tab_cp.wait()
-    hit = (lax.broadcasted_iota(jnp.int32, (reqs, steps), 1) == col[:, :1]).astype(F32)
-    picked = lax.dot_general(hit, tab_v[...], (((1,), (1,)), ((), ())), precision=HI, preferred_element_type=F32)
+    hit = jnp.where(lax.broadcasted_iota(jnp.int32, (reqs, steps), 1) == col[:, :1], 1.0, 0.0).astype(BF16)
+
+    def picked_of(part):
+        return lax.dot_general(hit, part, (((1,), (1,)), ((), ())), preferred_element_type=F32)
+
+    part_a = tab_v[...].astype(BF16)
+    rest = tab_v[...] - part_a.astype(F32)
+    part_b = rest.astype(BF16)
+    part_c = (rest - part_b.astype(F32)).astype(BF16)
+    picked = picked_of(part_a) + (picked_of(part_b) + picked_of(part_c))
     mod_src[...] = jnp.zeros_like(mod_src)
     for a in range(NZ):
         mod_src[a, :, : tab_v.shape[0]] = picked[a * ND : (a + 1) * ND]
@@ -116,7 +125,7 @@
         m1_copy(k, z).start()
         return c
 
-    lax.fori_loop(1, NZ, m1_start, 0)
+    lax.fori_loop(1, NZ, m1_start, 0, unroll=True)
     mod_all[z] = mod_src[z]
 
     def l1_wait(k, c):
@@ -140,7 +149,7 @@
         l2_copy(k, p).start()
         return c
 
-    lax.fori_loop(1, 2 * ND, l2_start, 0)
+    lax.fori_loop(1, 2 * ND, l2_start, 0, unroll=5)
     lat_recv[p] = lat_send[d]
 
     def m1_wait(k, c):
@@ -162,12 +171,22 @@
         m2_copy(k, p).start()
         return c
 
-    lax.fori_loop(1, 2 * ND, m2_start, 0)
+    lax.fori_loop(1, 2 * ND, m2_start, 0, unroll=5)
     mod_recv[p] = mod_send[d]
 
     emb_cp.wait()
     wbar = jnp.sum(emb_v[...].astype(F32), axis=1, keepdims=True) * (1.0 / feats)
-    wbar = jnp.broadcast_to(wbar, (wbar.shape[0], 128))
+    et = 256
+    tiles = feats // et
+
+    def gram_step(i, gram):
+        centred = emb_v[:, pl.ds(pl.multiple_of(i * et, et), et)].astype(F32) - wbar
+        return gram + lax.dot_general(
+            centred, centred, (((1,), (1,)), ((), ())), precision=HI, preferred_element_type=F32)
+
+    patch = emb_v.shape[0]
+    gram = lax.fori_loop(0, tiles, gram_step, jnp.zeros((patch, patch), F32), unroll=4) * (1.0 / feats)
+    wbar = jnp.broadcast_to(wbar, (patch, 128))
 
     def l2_wait(k, c):
         l2_copy(k, (p + k) % (2 * ND)).wait_recv()
@@ -180,28 +199,10 @@
             x = x + lat_recv[2 * b + t].astype(F32)
         xt[t * half : (t + 1) * half] = jnp.transpose(x).astype(BF16)
 
-    mean = lax.dot_general(xt[...].astype(F32), wbar, (((1,), (0,)), ((), ())), precision=HI, preferred_element_type=F32)
-    et = 256
-    tiles = feats // et
-    near_each = 10
-
-    def embed(t, n):
-        made = jnp.dot(xt[t * half : (t + 1) * half], emb_v[:, pl.ds(pl.multiple_of(n * et, et), et)],
-                       preferred_element_type=F32)
-        m = mean[t * half : (t + 1) * half]
-        return made[:, :128] - m, made[:, 128:] - m
-
-    def spread(t):
-        def body(i, ss):
-            for u in range(near_each):
-                c0, c1 = embed(t, i * near_each + u)
-                ss = ss + (c0 * c0 + c1 * c1)
-            return ss
-        ss = lax.fori_loop(0, tiles // near_each, body, jnp.zeros((half, 128), F32))
-        var = jnp.sum(ss, axis=1, keepdims=True) * (1.0 / feats)
-        return jnp.broadcast_to(1.0 / jnp.sqrt(var + EPS), (half, 128))
-
-    rstd = [spread(t) for t in range(2)]
+    xf = xt[...].astype(F32)
+    mean = jnp.dot(xf, wbar, precision=HI, preferred_element_type=F32)
+    var = jnp.sum(jnp.dot(xf, gram, precision=HI, preferred_element_type=F32) * xf, axis=1, keepdims=True)
+    rstd = jnp.broadcast_to(1.0 / jnp.sqrt(jnp.maximum(var, 0.0) + EPS), (tokens, 128))
 
     def m2_wait(k, c):
         m2_copy(k, (p + k) % (2 * ND)).wait_recv()
@@ -227,15 +228,17 @@
                 mod_row[c : c + 1, n : n + 128] = pieces[a][b : b + 1] + float(c)
 
     for t in range(2):
-        def body(i, c, t=t):
-            for u in range(near_each):
-                n = i * near_each + u
-                for h, v in enumerate(embed(t, n)):
-                    cols = pl.ds(pl.multiple_of(n * et + h * 128, 128), 128)
-                    v = v * rstd[t] * mod_row[1:2, cols] + mod_row[0:1, cols]
-                    normed[t * half : (t + 1) * half, cols] = v.astype(BF16)
+        rows_t = slice(t * half, (t + 1) * half)
+
+        def modulate(i, c, rows_t=rows_t):
+            made = jnp.dot(xt[rows_t], emb_v[:, pl.ds(pl.multiple_of(i * et, et), et)], preferred_element_type=F32)
+            for h in range(et // 128):
+                cols = pl.ds(pl.multiple_of(i * et + h * 128, 128), 128)
+                v = (made[:, h * 128 : (h + 1) * 128] - mean[rows_t]) * rstd[rows_t]
+                normed[rows_t, cols] = (v * mod_row[1:2, cols] + mod_row[0:1, cols]).astype(BF16)
             return c
-        lax.fori_loop(0, tiles // near_each, body, 0)
+
+        lax.fori_loop(0, tiles, modulate, 0, unroll=NORM)
 
     def arrive(base):
         def body(i, c):
@@ -286,6 +289,13 @@
 
     keypos = lax.broadcasted_iota(jnp.int32, (half, tokens), 1)
     rowpos = lax.broadcasted_iota(jnp.int32, (half, HD), 0)
+
+    def o_copy(i, side):
+        cols = pl.ds(pl.multiple_of(i * CW, CW), CW)
+        there = pl.ds(pl.multiple_of(side * width + i * CW, CW), CW)
+        return pltpu.make_async_remote_copy(
+            src_ref=out_far.at[:, cols], dst_ref=out_hbm.at[0, :, there], send_sem=o_send.at[i], recv_sem=o_recv.at[i],
+            device_id={"seq": 1 - s}, device_id_type=MESH)
 
     def attend(i, r0, out_ref, first):
         at = pl.ds(pl.multiple_of(r0, half), half)
@@ -306,21 +316,14 @@
             sc = jnp.where(keypos < live, sc * HD ** (-0.5), -jnp.inf)
             ex = jnp.exp(sc - jnp.max(sc, axis=1, keepdims=True))
             parts.append((ex * (1.0 / jnp.sum(ex, axis=1, keepdims=True))).astype(BF16))
-        for (n, hc, cols, _), pr in zip(work, parts):
+        for k, ((n, hc, cols, _), pr) in enumerate(zip(work, parts)):
             mixed = jnp.dot(pr, vbuf[n, :, hc], preferred_element_type=F32)
             out_ref[:, cols] = jnp.where(rowpos + r0 < shown, mixed, 0.0).astype(BF16)
-
-    def o_copy(i, side):
-        cols = pl.ds(pl.multiple_of(i * CW, CW), CW)
-        there = pl.ds(pl.multiple_of(side * width + i * CW, CW), CW)
-        return pltpu.make_async_remote_copy(
-            src_ref=out_far.at[:, cols], dst_ref=out_hbm.at[0, :, there], send_sem=o_send.at[i], recv_sem=o_recv.at[i],
-            device_id={"seq": 1 - s}, device_id_type=MESH)
+            if first and k % 2 == 1:
+                o_copy(n, s).start()
 
     def far(i, c):
         attend(i, (1 - s) * half, out_far, True)
-        for u in range(PAIRS):
-            o_copy(i * PAIRS + u, s).start()
         return c
 
     far(0, 0)

time: 51.9 us -> 49.4 us (0.952)
  Pallas kernels: 48.8 us -> 46.5 us
    pallas_call x1, Pallas kernels: 48.8 us -> 46.5 us  [per_device(): pl.pallas_call(kernel, out_shape=jax.ShapeDtypeStruct((1, half, 2 * width...]
where the time goes in v3:
time: 49.4 us; the launch traced here: 49.2 us
  Pallas kernels  46.5 us (94%)
  local copies, waits for them, and re-layouts  2.06 us (4%)
  between operations  0.66 us (1%)
    pallas_call x1, Pallas kernels, per_device(): pl.pallas_call(kernel, out_shape=jax.ShapeDtypeStruct((1, half, 2 * width...  46.5 us
    unnamed x1, local copies, waits for them, and re-layouts  2.06 us

profile of v3, /device:TPU:1, one launch (start us, length us, event | category | flops | bytes accessed | tf_op | source)
XLA Modules:
  0.0 49.2 jit_solution(4135406426245323344)
XLA Ops:
  0.7 46.5 %shard_map.91 = bf16[1,128,3072]{2,1,0:T(8,128)(2,1)} custom-call(s32[64]{0:T(128)} %order_s.1, s32[64]{0:T(128)} %time_s.1, s32[1]{0:T(128)S(6)} %copy.11.bound_s, s32[64]{0:T(128)} %len_s.1, bf16[1,64,128]{2,1,0:T(8,128)(2,1)} %lat_ref.1, f32[1,2,1536]{2,1,0:T(2,128)} %gain_ref.1, bf16[1,64,5120]{2,1,0:T(8,128)(2,1)} %emb_hbm.1, f32[80,1024]{1,0:T(8,128)} %bitcast.9, ...), custom_call_target="tpu_custom_call" | custom-call | flops 12999999488 | bytes 49000000 | tf_op jit(solution)/shard_map/pallas_call | solution.py:378
  47.2 2.1 %copy.12 = bf16[1,128,3072]{2,1,0:T(8,128)(2,1)} copy(bf16[1,128,3072]{2,1,0:T(8,128)(2,1)} %shard_map.91) | data formatting | bytes 1572864

commit v4 on v3

--- a/solution.py
+++ b/solution.py
@@ -1,3 +1,5 @@
+import functools
+
 import jax
 import jax.numpy as jnp
 from jax import lax
@@ -16,15 +18,16 @@
 HI = lax.Precision.HIGHEST
 UNROLL = 6
 NORM = 20
+SLOTS = 14
 PAIRS = 3
 
 
 def kernel(
-    order_s, time_s, bound_s, len_s, lat_ref, gain_ref, emb_hbm, tab_hbm, w_hbm,
+    order_hbm, time_hbm, bound_s, len_hbm, lat_hbm, gain_hbm, emb_hbm, tab_hbm, w_hbm,
     out_hbm,
-    emb_v, tab_v, wbuf,
+    order_s, time_s, len_s, lat_ref, gain_ref, emb_v, tab_v, wbuf,
     lat_all, lat_send, lat_recv, mod_src, mod_all, mod_send, mod_recv, mod_row,
-    xt, normed, proj, vbuf, kbuf, sq_send, sq_recv, inv_qk, out_far, out_own,
+    right_v, xt, normed, proj, vbuf, kbuf, sq_send, sq_recv, inv_qk, out_far, out_own,
     loc_sem, w_sem, l1_send, l1_recv, m1_send, m1_recv, l2_send, l2_recv, m2_send, m2_recv,
     sq_sem, o_send, o_recv,
 ):
@@ -43,20 +46,28 @@
 
     emb_cp = pltpu.make_async_copy(emb_hbm.at[0], emb_v, loc_sem.at[0])
     tab_cp = pltpu.make_async_copy(tab_hbm, tab_v, loc_sem.at[1])
+    small = [
+        pltpu.make_async_copy(src, dst, loc_sem.at[3 + k])
+        for k, (src, dst) in enumerate([
+            (lat_hbm, lat_ref), (order_hbm, order_s), (time_hbm, time_s), (len_hbm, len_s), (gain_hbm, gain_ref)])
+    ]
+    for cp in small[:4]:
+        cp.start()
     tab_cp.start()
     emb_cp.start()
+    small[4].start()
 
     def w_copy(i):
         return pltpu.make_async_copy(
             w_hbm.at[i // chunks, :, pl.ds(pl.multiple_of((i % chunks) * CW, CW), CW)],
-            wbuf.at[i], w_sem.at[i],
+            wbuf.at[i % SLOTS], w_sem.at[i],
         )
 
     def w_start(i, c):
         w_copy(i).start()
         return c
 
-    lax.fori_loop(0, 3 * chunks, w_start, 0)
+    lax.fori_loop(0, SLOTS, w_start, 0)
 
     barrier = pltpu.get_barrier_semaphore()
 
@@ -72,6 +83,8 @@
     lax.fori_loop(1, NZ, greet_z, 0)
     lax.fori_loop(1, 2 * ND, greet_p, 0)
     pl.semaphore_wait(barrier, NZ - 1 + 2 * ND - 1)
+
+    small[0].wait()
 
     def l1_copy(k, slot):
         return pltpu.make_async_remote_copy(
@@ -84,6 +97,9 @@
 
     lax.fori_loop(1, NZ, l1_start, 0, unroll=True)
     lat_all[z] = lat_ref[0]
+
+    for cp in small[1:4]:
+        cp.wait()
 
     rows = lax.broadcasted_iota(jnp.int32, (reqs, 128), 0)
 
@@ -186,7 +202,11 @@
 
     patch = emb_v.shape[0]
     gram = lax.fori_loop(0, tiles, gram_step, jnp.zeros((patch, patch), F32), unroll=4) * (1.0 / feats)
-    wbar = jnp.broadcast_to(wbar, (patch, 128))
+    right = jnp.concatenate([jnp.broadcast_to(wbar, (patch, 128)), gram, jnp.zeros((patch, 128 - patch), F32)], axis=1)
+    for k in range(3):
+        part = right.astype(BF16)
+        right_v[k] = part
+        right = right - part.astype(F32)
 
     def l2_wait(k, c):
         l2_copy(k, (p + k) % (2 * ND)).wait_recv()
@@ -199,9 +219,11 @@
             x = x + lat_recv[2 * b + t].astype(F32)
         xt[t * half : (t + 1) * half] = jnp.transpose(x).astype(BF16)
 
-    xf = xt[...].astype(F32)
-    mean = jnp.dot(xf, wbar, precision=HI, preferred_element_type=F32)
-    var = jnp.sum(jnp.dot(xf, gram, precision=HI, preferred_element_type=F32) * xf, axis=1, keepdims=True)
+    xb = xt[...]
+    both = [jnp.dot(xb, right_v[k], preferred_element_type=F32) for k in range(3)]
+    both = both[0] + (both[1] + both[2])
+    mean = both[:, :128]
+    var = jnp.sum(both[:, 128 : 128 + patch] * xb.astype(F32), axis=1, keepdims=True)
     rstd = jnp.broadcast_to(1.0 / jnp.sqrt(jnp.maximum(var, 0.0) + EPS), (tokens, 128))
 
     def m2_wait(k, c):
@@ -227,27 +249,27 @@
                 n = (b * span + a) * 128
                 mod_row[c : c + 1, n : n + 128] = pieces[a][b : b + 1] + float(c)
 
-    for t in range(2):
-        rows_t = slice(t * half, (t + 1) * half)
-
-        def modulate(i, c, rows_t=rows_t):
-            made = jnp.dot(xt[rows_t], emb_v[:, pl.ds(pl.multiple_of(i * et, et), et)], preferred_element_type=F32)
+    def arrive(i, c):
+        w_copy(i).wait()
+        return c
+
+    lax.fori_loop(0, chunks, arrive, 0)
+
+    def modulate(i, c):
+        tile = pl.ds(pl.multiple_of(i * et, et), et)
+        for t in range(2):
+            rows_t = slice(t * half, (t + 1) * half)
+            made = jnp.dot(xt[rows_t], emb_v[:, tile], preferred_element_type=F32)
             for h in range(et // 128):
                 cols = pl.ds(pl.multiple_of(i * et + h * 128, 128), 128)
                 v = (made[:, h * 128 : (h + 1) * 128] - mean[rows_t]) * rstd[rows_t]
                 normed[rows_t, cols] = (v * mod_row[1:2, cols] + mod_row[0:1, cols]).astype(BF16)
-            return c
-
-        lax.fori_loop(0, tiles, modulate, 0, unroll=NORM)
-
-    def arrive(base):
-        def body(i, c):
-            w_copy(base + i).wait()
-            return c
-        lax.fori_loop(0, chunks, body, 0)
+        return c
+
+    lax.fori_loop(0, tiles, modulate, 0, unroll=NORM)
 
     def project(i):
-        return jnp.dot(normed[...], wbuf[i], preferred_element_type=F32)
+        return jnp.dot(normed[...], wbuf[i % SLOTS], preferred_element_type=F32)
 
     def squares(base):
         def body(i, ss):
@@ -262,9 +284,9 @@
     def as_rows(ss):
         return lax.dot_general(ones, ss, (((1,), (1,)), ((), ())), precision=HI, preferred_element_type=F32)
 
-    arrive(0)
     q_ss = squares(0)
-    arrive(chunks)
+    lax.fori_loop(SLOTS, 3 * chunks, w_start, 0)
+    lax.fori_loop(chunks, 2 * chunks, arrive, 0)
     k_ss = squares(chunks)
     sq_send[0] = as_rows(q_ss)
     sq_send[1] = as_rows(k_ss)
@@ -278,8 +300,9 @@
         return c
 
     first = chunks // 2
-    arrive(2 * chunks)
-    lax.fori_loop(0, first, values, 0, unroll=UNROLL)
+    lax.fori_loop(2 * chunks, 3 * chunks, arrive, 0)
+    small[4].wait()
+    lax.fori_loop(0, first, values, 0, unroll=first)
     sq_cp.wait_recv()
     for c in range(2):
         total = sq_send[c] + sq_recv[c]
@@ -327,7 +350,7 @@
         return c
 
     far(0, 0)
-    lax.fori_loop(first, chunks, values, 0, unroll=UNROLL)
+    lax.fori_loop(first, chunks, values, 0, unroll=first)
     far(1, 0)
 
     def near(i, c):
@@ -371,19 +394,25 @@
     table = jnp.transpose(mod_table[0], (1, 2, 0)).reshape(-1, steps)
     weights = jnp.transpose(qkv_weight[0], (1, 0, 2))
     tokens, half = 256, 128
+    keep = functools.partial(pltpu.with_memory_space_constraint, memory_space=pltpu.HBM)
     smem = pl.BlockSpec(memory_space=pltpu.SMEM)
-    vmem = pl.BlockSpec(memory_space=pltpu.VMEM)
+    hbm = pl.BlockSpec(memory_space=pltpu.HBM)
     anywhere = pl.BlockSpec(memory_space=pl.ANY)
     dma = pltpu.SemaphoreType.DMA
     return pl.pallas_call(
         kernel,
         out_shape=jax.ShapeDtypeStruct((1, half, 2 * width), BF16),
-        in_specs=[smem] * 4 + [vmem] * 2 + [anywhere] * 3,
+        in_specs=[hbm] * 2 + [smem] + [hbm] * 6,
         out_specs=anywhere,
         scratch_shapes=[
+            pltpu.SMEM(order.shape, jnp.int32),
+            pltpu.SMEM(timestep.shape, jnp.int32),
+            pltpu.SMEM(lengths.shape, jnp.int32),
+            pltpu.VMEM(latents.shape, BF16),
+            pltpu.VMEM(qk_gain.shape, F32),
             pltpu.VMEM((patch, feats), BF16),
             pltpu.VMEM(table.shape, F32),
-            pltpu.VMEM((3 * chunks, feats, CW), BF16),
+            pltpu.VMEM((SLOTS, feats, CW), BF16),
             pltpu.VMEM((NZ, patch, half), BF16),
             pltpu.VMEM((ND, patch, half), BF16),
             pltpu.VMEM((2 * ND, patch, half), BF16),
@@ -392,6 +421,7 @@
             pltpu.VMEM((ND, NZ, 128), F32),
             pltpu.VMEM((2 * ND, NZ, 128), F32),
             pltpu.VMEM((2, feats), F32),
+            pltpu.VMEM((3, patch, 256), BF16),
             pltpu.VMEM((tokens, patch), BF16),
             pltpu.VMEM((tokens, feats), BF16),
             pltpu.VMEM((2 * chunks, tokens, CW), F32),
@@ -402,7 +432,7 @@
             pltpu.VMEM((2, tokens, 128), F32),
             pltpu.VMEM((half, width), BF16),
             pltpu.VMEM((half, width), BF16),
-            dma((3,)),
+            dma((8,)),
             dma((3 * chunks,)),
             dma((NZ,)), dma((NZ,)), dma((NZ,)), dma((NZ,)),
             dma((2 * ND,)), dma((2 * ND,)), dma((2 * ND,)), dma((2 * ND,)),
@@ -410,9 +440,10 @@
             dma((chunks,)), dma((chunks,)),
         ],
         compiler_params=pltpu.CompilerParams(
-            collective_id=0, has_side_effects=True, vmem_limit_bytes=57 * 1024 * 1024),
+            collective_id=0, has_side_effects=True, vmem_limit_bytes=48 * 1024 * 1024),
         cost_estimate=pl.CostEstimate(flops=13 * 10**9, bytes_accessed=49 * 10**6, transcendentals=800000),
-    )(order, timestep, boundary, lengths, latents, qk_gain, embed_weight, table, weights)
+    )(keep(order), keep(timestep), boundary, keep(lengths), keep(latents), keep(qk_gain), keep(embed_weight),
+      keep(table), keep(weights))
 
 
 def solution(mesh):

time: 49.4 us -> 47.3 us (0.957)
  local copies, waits for them, and re-layouts: 2.06 us -> 0.88 us
  Pallas kernels: 46.5 us -> 45.6 us
    unnamed x1, local copies, waits for them, and re-layouts: 2.06 us -> 0.88 us
    pallas_call x1, Pallas kernels: 46.5 us -> 45.6 us  [per_device(): pl.pallas_call(kernel, out_shape=jax.ShapeDtypeStruct((1, half, 2 * width...]
where the time goes in v4:
time: 47.3 us; the launch traced here: 47.2 us
  Pallas kernels  45.6 us (96%)
  local copies, waits for them, and re-layouts  0.88 us (2%)
  between operations  0.66 us (1%)
    pallas_call x1, Pallas kernels, per_device(): pl.pallas_call(kernel, out_shape=jax.ShapeDtypeStruct((1, half, 2 * width...  45.6 us

profile of v4, /device:TPU:1, one launch (start us, length us, event | category | flops | bytes accessed | tf_op | source)
XLA Modules:
  0.0 47.2 jit_solution(3626647394193372589)
XLA Ops:
  0.7 45.6 %shard_map.91 = bf16[1,128,3072]{2,1,0:T(8,128)(2,1)S(1)} custom-call(s32[64]{0:T(128)} %order_hbm.1, s32[64]{0:T(128)} %time_hbm.1, s32[1]{0:T(128)S(6)} %copy.11.bound_s, s32[64]{0:T(128)} %len_hbm.1, bf16[1,64,128]{2,1,0:T(8,128)(2,1)} %lat_hbm.1, f32[1,2,1536]{2,1,0:T(2,128)} %gain_hbm.1, bf16[1,64,5120]{2,1,0:T(8,128)(2,1)} %emb_hbm.1, ...), custom_call_target="tpu_custom_call" | custom-call | flops 12999999488 | bytes 49000000 | tf_op jit(solution)/shard_map/pallas_call | solution.py:402
  46.3 0.9 %copy.12 = bf16[1,128,3072]{2,1,0:T(8,128)(2,1)} copy(bf16[1,128,3072]{2,1,0:T(8,128)(2,1)S(1)} %shard_map.91) | data formatting | bytes 1572864

commit v5 on v4

--- a/solution.py
+++ b/solution.py
@@ -67,7 +67,6 @@
         w_copy(i).start()
         return c
 
-    lax.fori_loop(0, SLOTS, w_start, 0)
 
     barrier = pltpu.get_barrier_semaphore()
 
@@ -82,7 +81,7 @@
 
     lax.fori_loop(1, NZ, greet_z, 0)
     lax.fori_loop(1, 2 * ND, greet_p, 0)
-    pl.semaphore_wait(barrier, NZ - 1 + 2 * ND - 1)
+    lax.fori_loop(0, SLOTS, w_start, 0)
 
     small[0].wait()
 
@@ -95,7 +94,6 @@
         l1_copy(k, z).start()
         return c
 
-    lax.fori_loop(1, NZ, l1_start, 0, unroll=True)
     lat_all[z] = lat_ref[0]
 
     for cp in small[1:4]:
@@ -130,6 +128,9 @@
     mod_src[...] = jnp.zeros_like(mod_src)
     for a in range(NZ):
         mod_src[a, :, : tab_v.shape[0]] = picked[a * ND : (a + 1) * ND]
+
+    pl.semaphore_wait(barrier, NZ - 1 + 2 * ND - 1)
+    lax.fori_loop(1, NZ, l1_start, 0, unroll=True)
 
     def m1_copy(k, slot):
         z2 = (z + k) % NZ

time: 47.3 us -> 47.2 us (level)
  no operation moved by 1% of the time
where the time goes in v5:
time: 47.2 us; the launch traced here: 47.1 us
  Pallas kernels  45.5 us (96%)
  local copies, waits for them, and re-layouts  0.88 us (2%)
  between operations  0.66 us (1%)
    pallas_call x1, Pallas kernels, per_device(): pl.pallas_call(kernel, out_shape=jax.ShapeDtypeStruct((1, half, 2 * width...  45.5 us

profile of v5, /device:TPU:1, one launch (start us, length us, event | category | flops | bytes accessed | tf_op | source)
XLA Modules:
  0.0 47.1 jit_solution(11911596881640012686)
XLA Ops:
  0.7 45.5 %shard_map.91 = bf16[1,128,3072]{2,1,0:T(8,128)(2,1)S(1)} custom-call(s32[64]{0:T(128)} %order_hbm.1, s32[64]{0:T(128)} %time_hbm.1, s32[1]{0:T(128)S(6)} %copy.11.bound_s, s32[64]{0:T(128)} %len_hbm.1, bf16[1,64,128]{2,1,0:T(8,128)(2,1)} %lat_hbm.1, f32[1,2,1536]{2,1,0:T(2,128)} %gain_hbm.1, bf16[1,64,5120]{2,1,0:T(8,128)(2,1)} %emb_hbm.1, ...), custom_call_target="tpu_custom_call" | custom-call | flops 12999999488 | bytes 49000000 | tf_op jit(solution)/shard_map/pallas_call | solution.py:403
  46.2 0.9 %copy.12 = bf16[1,128,3072]{2,1,0:T(8,128)(2,1)} copy(bf16[1,128,3072]{2,1,0:T(8,128)(2,1)S(1)} %shard_map.91) | data formatting | bytes 1572864
